TPU v7x, 32 devices: a whole 2x2x4 slice. The times are simulated.
32 devices in a mesh: head: 8 (over z, y), ctx: 4 (over x, core).
Axes of the slice: x: 2, y: 2, z: 4, core: 2. Of those that a mesh axis runs over, the one named last changes fastest.
Arguments:
- queries: bfloat16 [1024, 2048], P(('ctx', 'head')), may hold values from -9 to 9
- keys: bfloat16 [1024, 8192], P('ctx', 'head'), may hold values from -9 to 9
- values: bfloat16 [1024, 8192], P('ctx', 'head'), may hold values from -6 to 6
- routes: int32 [1024, 16], P(('ctx', 'head')), may hold values from 0 to 63, all different within a row; in each aligned block of 32 rows (0 to 31, 32 to 63, ...) at most 16 rows name the same one
- gates: float32 [1024, 16], P(('ctx', 'head')), may hold values from 0.25 to 1
- block_mask: int32 [8, 8], replicated, may hold values 0 or 1
- w_out: bfloat16 [8192, 8192], P('head'), may hold values from -0.125 to 0.125
Outputs:
- mixed: bfloat16 [1024, 8192], P(('ctx', 'head'))
Inputs may be any that keep to these rules, and one draw needn't show every extreme that they name: `routes`: in each aligned block of 32 rows (the rows of one device) no head is named more than 16 times; each row names 16 different heads.
All inputs are finite; a program needn't handle non-finite values.
Results may differ from a plain program's by a relative error of at most 0.015.
Values may be sent and summed in bfloat16 or wider, within the bound.
A program may use at most 128 MiB of HBM per device.

v0:
```python
import math

import jax
import jax.numpy as jnp
from jax import lax
from jax.sharding import PartitionSpec as P

H = 64
HD = 128
BLK = 128
CAP = 16


def local(queries, keys, values, routes, gates, block_mask, w_out):
    tok_dev, routed = routes.shape
    ctx_tok = keys.shape[0]
    per_dev = keys.shape[1] // HD
    head_count = lax.axis_size("head")
    ctx_count = lax.axis_size("ctx")
    seq_len = ctx_tok * ctx_count
    slot_count = head_count * CAP
    head_ids = jnp.arange(H, dtype=jnp.int32)
    onehot = (routes[:, :, None] == head_ids[None, None, :]).astype(jnp.int32)
    per_token = jnp.sum(onehot, axis=1)
    earlier = jnp.cumsum(per_token, axis=0) - per_token
    ranking = jnp.sum(onehot * earlier[:, None, :], axis=2)
    target = (routes * CAP + ranking).reshape(-1)
    select = (jnp.arange(H * CAP, dtype=jnp.int32)[:, None] == target[None, :]).astype(jnp.bfloat16)
    packed = jnp.dot(
        select, queries.reshape(tok_dev * routed, HD), preferred_element_type=jnp.float32
    ).astype(jnp.bfloat16)
    packed = packed.reshape(head_count, per_dev, CAP, HD)
    arrived = lax.all_to_all(packed, "head", split_axis=0, concat_axis=2, tiled=True).reshape(
        per_dev, slot_count, HD
    )
    group_routes, group_gates = (
        lax.all_gather(routes, "head", axis=0, tiled=True),
        lax.all_gather(gates, "head", axis=0, tiled=True),
    )
    own_heads = lax.axis_index("head") * per_dev + jnp.arange(per_dev, dtype=jnp.int32)
    chosen = (group_routes[:, :, None] == own_heads[None, None, :]).astype(jnp.int32)
    token_hit = jnp.sum(chosen, axis=1)
    token_gate = jnp.sum(chosen.astype(jnp.float32) * group_gates[:, :, None], axis=1)
    block_hit = token_hit.reshape(head_count, tok_dev, per_dev)
    block_rank = jnp.cumsum(block_hit, axis=1) - block_hit
    placed = block_hit[..., None] * (
        block_rank[..., None] == jnp.arange(CAP, dtype=jnp.int32)
    ).astype(jnp.int32)
    diagonal = jnp.eye(head_count, dtype=jnp.int32)
    mapping = placed.transpose(2, 0, 1, 3)[:, :, :, None, :] * diagonal[None, :, None, :, None]
    mapping = mapping.reshape(per_dev, ctx_tok, slot_count)
    slot_token = jnp.sum(mapping * jnp.arange(ctx_tok, dtype=jnp.int32)[None, :, None], axis=1)
    slot_gate = jnp.sum(mapping.astype(jnp.float32) * token_gate.T[:, :, None], axis=1)
    ctx_index = lax.axis_index("ctx")
    query_pos = ctx_index * ctx_tok + slot_token
    blocks = seq_len // BLK
    block_ids = jnp.arange(blocks, dtype=jnp.int32)
    usable = (block_ids[None, :] < block_ids[:, None]) & (block_mask == 1) | (
        block_ids[None, :] == block_ids[:, None]
    )
    query_rows = usable[query_pos // BLK]
    score_scale = 1.0 / math.sqrt(HD)
    start_state = (
        jnp.full((per_dev, slot_count), -1e30, jnp.float32),
        jnp.zeros((per_dev, slot_count), jnp.float32),
        jnp.zeros((per_dev, slot_count, HD), jnp.float32),
    )

    def update(carried, key_block, value_block, key_pos):
        allowed = jnp.take(query_rows, key_pos // BLK, axis=2) & (
            key_pos[None, None, :] <= query_pos[:, :, None]
        )
        peak, total, summed = carried
        scores = (
            jnp.einsum("pqd,kpd->pqk", arrived, key_block, preferred_element_type=jnp.float32)
            * score_scale
        )
        masked = jnp.where(allowed, scores, -1e30)
        new_peak = jnp.maximum(peak, jnp.max(masked, axis=2))
        factor = jnp.exp(peak - new_peak)
        weights = jnp.where(allowed, jnp.exp(scores - new_peak[..., None]), 0.0)
        total = total * factor + jnp.sum(weights, axis=2)
        summed = summed * factor[..., None] + jnp.einsum(
            "pqk,kpd->pqd",
            weights.astype(jnp.bfloat16),
            value_block,
            preferred_element_type=jnp.float32,
        )
        return (new_peak, total, summed)

    key_value = jnp.stack((keys, values))
    piece_pair = lax.all_gather(key_value, "ctx", axis=1, tiled=True)
    length = piece_pair.shape[1]
    block_len = 512
    reshaped = piece_pair.reshape(2, length, per_dev, HD)

    def sub_block(index, current):
        window = lax.dynamic_slice_in_dim(reshaped, index * block_len, block_len, 1)
        key_pos = index * block_len + jnp.arange(block_len, dtype=jnp.int32)
        return update(current, window[0], window[1], key_pos)

    carried = lax.fori_loop(0, length // block_len, sub_block, start_state)
    peak, total, summed = carried
    attended = (summed / total[..., None] * slot_gate[..., None]).astype(jnp.bfloat16)
    weighted = jnp.einsum(
        "ptq,pqd->tpd", mapping.astype(jnp.bfloat16), attended, preferred_element_type=jnp.float32
    )
    weighted = weighted.astype(jnp.bfloat16).reshape(ctx_tok, per_dev * HD)
    return lax.psum_scatter(
        jnp.dot(weighted, w_out, preferred_element_type=jnp.float32).astype(jnp.bfloat16),
        "head",
        scatter_dimension=0,
        tiled=True,
    )


def solution(mesh):
    placed = (
        P(("ctx", "head"), None),
        P("ctx", "head"),
        P("ctx", "head"),
        P(("ctx", "head"), None),
        P(("ctx", "head"), None),
        P(),
        P("head", None),
    )
    return jax.shard_map(
        local, mesh=mesh, in_specs=placed, out_specs=P(("ctx", "head"), None), check_vma=False
    )
```

profile of v0, /device:TPU:2, one launch (start us, length us, event | category | flops | bytes accessed | tf_op | source)
XLA Modules:
  0.0 241.6 jit_solution(15929142443096106847)
XLA Ops:
  6.5 1.2 copy.57
  7.8 1.3 copy.58
  9.1 1.1 pad_maximum_fusion
  10.3 0.2 convert_reduce_fusion
  10.5 0.7 select_reduce_fusion
  11.4 1.2 fusion.22
  12.6 6.0 %all-to-all-start = ((bf16[8,8,16,128]{3,2,1,0:T(8,128)(2,1)}), bf16[8,8,16,128]{3,2,1,0:T(8,128)(2,1)S(1)}, u32[]{:S(2)}, u32[]{:S(2)}) async-start(bf16[8,8,16,128]{3,2,1,0:T(8,128)(2,1)} %bitcast.8), calls=%async_computation | async-start | bytes 524288 | tf_op jit(solution)/shard_map/all_to_all | solution.py:33
  18.6 32.9 %all-gather = s32[8,32,16]{1,2,0:T(8,128)S(1)} all-gather(s32[1,32,16]{1,2,0:T(8,128)S(1)} %bitcast.103), channel_id=1, replica_groups=mesh['head'=8,'ctx'=4] {'head'}, dimensions={0}, use_global_device_ids=true | all-gather | bytes 18432 | tf_op jit(solution)/shard_map/all_gather | solution.py:37
  51.7 0.1 copy.54
  51.9 2.1 fusion.23
  54.0 0.1 copy.56
  54.1 18.2 %fusion.18 = s32[8,8,16]{2,1,0:T(8,128)S(1)} fusion(s32[8,32]{1,0:T(8,128)S(1)} %multiply_add_fusion.1, s32[8,8]{0,1:T(8,128)S(1)} %fusion.36, s32[8,8,32,16]{2,1,3,0:T(8,128)S(1)} %fusion.26), kind=kLoop, calls=%fused_computation.47 | loop fusion | flops 785408 | bytes 136448 | tf_op jit(solution)/shard_map/reduce_sum | solution.py:52
  72.6 3.2 %gather_fusion.1 = pred[1024,8]{1,0:T(8,128)(4,1)S(1)} fusion(pred[8,8]{1,0:T(8,128)(4,1)S(1)} %fusion.35, s32[1024]{0:T(1024)S(1)} %fusion.33), kind=kCustom, calls=%fused_computation.1 | custom fusion | bytes 20480 | tf_op jit(solution)/shard_map/gather | solution.py:61
  75.8 0.2 copy.62
  76.0 30.5 %all-gather.1 = f32[8,32,16]{1,2,0:T(8,128)S(1)} all-gather(f32[1,32,16]{1,2,0:T(8,128)S(1)} %bitcast.105), channel_id=1, replica_groups=mesh['head'=8,'ctx'=4] {'head'}, dimensions={0}, use_global_device_ids=true | all-gather | bytes 18432 | tf_op jit(solution)/shard_map/all_gather | solution.py:38
  106.8 2.4 fusion.20
  109.2 2.5 %mul.165 = s32[8,8,32,8,16]{2,1,4,3,0:T(8,128)} broadcast(s32[8,8,32,16]{2,1,3,0:T(8,128)S(1)} %fusion.26), dimensions={0,1,2,4} | broadcast | bytes 1179648 | tf_op jit(solution)/shard_map/mul | solution.py:50
  111.7 4.2 %mul.185 = s32[8,256,128]{1,2,0:T(8,128)} reshape(s32[8,8,32,8,16]{2,1,4,3,0:T(8,128)} %mul.165) | data formatting | bytes 2097152 | tf_op jit(solution)/shard_map/mul | solution.py:50
  115.9 0.1 mul.186
  116.0 0.2 mul.187
  116.2 17.2 %while.20 = (s32[]{:T(128)}, f32[8,128]{1,0:T(8,128)S(1)}, f32[8,128]{1,0:T(8,128)S(1)}, f32[8,128,128]{2,1,0:T(8,128)}, pred[8,128,8]{1,0,2:T(8,128)(4,1)S(1)},...) while((s32[]{:T(128)}, f32[8,128]{1,0:T(8,128)S(1)}, ...), condition=%wide.region_9.10_spmd.clone, body=%wide.region_6.9_spmd.clone.sunk | while | flops 279342080 | bytes 12419291 | solution.py:102
  116.3 1.8 gather_fusion
  118.2 2.4 fusion.50
  120.6 0.9 fusion.51
  121.5 3.3 %convolution_add_fusion.2 = f32[8,128,128]{2,1,0:T(8,128)} fusion(f32[8,512,128]{2,1,0:T(8,128)S(1)} %get-tuple-element.340, bf16[2,1024,8,128]{1,3,2,0:T(8,128)(2,1)} %get-tuple-element.375, s32[]{:T(128)S(6)} %add.298, s32[]{:T(128)S(6)} %select_n.194, f32[8,128]{1,0:T(8,128)S(1)} %select_maximum_fusion.2, f32[8,128,128]{2,1,0:T(8,128)} %get-tuple-element.359, ...), kind=kOutput, calls=%fused_computation.11.clone.1 | convolution fusion | flops 138280960 | bytes 4733449 | tf_op jit(solution)/shard_map/while/body/eval_jaxpr/pqk,kpd->pqd/dot_general | solution.py:83
  124.8 1.8 gather_fusion
  126.7 2.4 fusion.50
  129.1 0.9 fusion.51
  130.0 3.4 %convolution_add_fusion.2 = f32[8,128,128]{2,1,0:T(8,128)} fusion(f32[8,512,128]{2,1,0:T(8,128)S(1)} %get-tuple-element.340, bf16[2,1024,8,128]{1,3,2,0:T(8,128)(2,1)} %get-tuple-element.375, s32[]{:T(128)S(6)} %add.298, s32[]{:T(128)S(6)} %select_n.194, f32[8,128]{1,0:T(8,128)S(1)} %select_maximum_fusion.2, f32[8,128,128]{2,1,0:T(8,128)} %get-tuple-element.359, ...), kind=kOutput, calls=%fused_computation.11.clone.1 | convolution fusion | flops 138280960 | bytes 4733449 | tf_op jit(solution)/shard_map/while/body/eval_jaxpr/pqk,kpd->pqd/dot_general | solution.py:83
  133.5 2.0 convolution_convert_fusion.1
  135.5 12.1 %convolution_convert_fusion = bf16[256,8192]{1,0:T(8,128)(2,1)} fusion(bf16[256,1024]{0,1:T(8,128)(2,1)S(1)} %bitcast.99, bf16[1024,8192]{1,0:T(8,128)(2,1)} %param.15), kind=kOutput, calls=%fused_computation.44 | convolution fusion | flops 4297064448 | bytes 21495808 | tf_op jit(solution)/shard_map/dot_general | solution.py:110
  147.6 87.2 %reduce-scatter.2.cloned.1.call-done = bf16[32,8192]{1,0:T(8,128)(2,1)} async-done(((bf16[256,8192]{1,0:T(8,128)(2,1)}), bf16[32,8192]{1,0:T(8,128)(2,1)}) %reduce-scatter.2.cloned.1.call-update) | async-done | bytes 524304 | tf_op jit(solution)/shard_map/reduce_scatter | solution.py:109
  (56 shorter events, 1.4 us)
Async XLA Ops:
  6.5 109.7 %all-gather.4.cloned.1.call-start = ((), (), s32[]{:S(2)}) async-start(), calls=%async_computation.2 | async-start | bytes 5242880 | tf_op jit(solution)/shard_map/all_gather | solution.py:92
  7.8 2.4 copy-start.1
  7.8 3.5 %copy-start = (bf16[32,2048]{1,0:T(8,128)(2,1)S(1)}, bf16[32,2048]{1,0:T(8,128)(2,1)}, u32[]{:S(2)}) copy-start(bf16[32,2048]{1,0:T(8,128)(2,1)} %param.9) | copy-start | bytes 393220
  11.2 61.2 %copy-start.3 = (s32[8,8]{1,0:T(8,128)S(1)}, s32[8,8]{1,0:T(8,128)}, u32[]{:S(2)}) copy-start(s32[8,8]{1,0:T(8,128)} %param.14) | copy-start | bytes 772
  12.6 63.4 %copy-start.2 = (f32[32,16]{0,1:T(8,128)S(1)}, f32[32,16]{0,1:T(8,128)}, u32[]{:S(2)}) copy-start(f32[32,16]{0,1:T(8,128)} %param.13) | copy-start | bytes 6148
  12.6 103.6 %all-to-all-start = ((bf16[8,8,16,128]{3,2,1,0:T(8,128)(2,1)}), bf16[8,8,16,128]{3,2,1,0:T(8,128)(2,1)S(1)}, u32[]{:S(2)}, u32[]{:S(2)}) async-start(bf16[8,8,16,128]{3,2,1,0:T(8,128)(2,1)} %bitcast.8), calls=%async_computation | async-start | bytes 524288 | tf_op jit(solution)/shard_map/all_to_all | solution.py:33
  18.5 216.3 %reduce-scatter.2.cloned.1.call-start = ((), (), s32[]{:S(2)}) async-start(), calls=%async_computation.3 | async-start | bytes 4718592 | tf_op jit(solution)/shard_map/reduce_scatter | solution.py:109
Sparse Core Ops, SparseCore 0:
  10.3 35.0 all-gather.3
  147.7 87.0 reduce-scatter.1
where the time goes:
time: 244 us; the launch traced here: 242 us
  waiting for transfers between devices  87.3 us (36%)
  blocking collectives  63.4 us (26%)
  other arithmetic  26.8 us (11%)
  matrix products  26.8 us (11%)
  local copies, waits for them, and re-layouts  17.6 us (7%)
  between operations  13.6 us (6%)
  starting transfers between devices  6.01 us (2%)
    reduce_scatter x1, waiting for transfers between devices, local(): lax.psum_scatter(jnp.dot(weighted, w_out, preferred_element_type=jnp.floa...  87.2 us
    all_gather x1, blocking collectives, local(): lax.all_gather(routes, 'head', axis=0, tiled=True)  32.9 us
    all_gather x1, blocking collectives, local(): lax.all_gather(gates, 'head', axis=0, tiled=True)  30.5 us
    reduce_sum x1, other arithmetic, local(): jnp.sum(mapping * jnp.arange(ctx_tok, dtype=jnp.int32)[None, :, None], ax...  18.2 us
    dot_general x1, matrix products, local(): jnp.dot(weighted, w_out, preferred_element_type=jnp.float32)  12.1 us
    mul x4, local copies, waits for them, and re-layouts, local(): placed.transpose(2, 0, 1, 3)[:, :, :, None, :]  6.94 us
    dot_general x2, matrix products, update(): jnp.einsum('pqk,kpd->pqd', weights.astype(jnp.bfloat16), value_block, pre...  6.75 us
    all_to_all x1, starting transfers between devices, local(): lax.all_to_all(packed, 'head', split_axis=0, concat_axis=2, tiled=True)  5.97 us
  transfers between devices with their start and end apart: 3, of which 1 were waited for; matrix products, arithmetic and copies ran while one was open for 15% of the time, Pallas kernels for 0%

commit v1 on v0

v1 whole, which is shorter than its diff:
```python
import functools
import math

import jax
import jax.numpy as jnp
from jax import lax
from jax.experimental import pallas as pl
from jax.experimental.pallas import tpu as pltpu
from jax.sharding import PartitionSpec as P

HD = 128
BLK = 128
CHUNK = 512
MESH = pl.DeviceIdType.MESH


def kernel(
    n, ctxs,
    queries_ref, keys_ref, values_ref, routes_ref, gates_ref, mask_ref, w_hbm,
    out_ref,
    qf, rb, gb, qsend, gsend, qall, gall, kv, bias, weighted, w_ref,
    ysend, yrecv, psum, zrecv,
    w_sem, own_sem, x_send, x_recv, s_send, s_recv, q_send, q_recv, g_send, g_recv,
    y_send, y_recv, up_send, up_recv, dn_send, dn_recv,
):
    me = lax.axis_index("head")
    cx = lax.axis_index("ctx")
    y, z, m = lax.rem(me, 2), me // 2, n // 2
    core, chip, chips = lax.rem(cx, 2), cx // 2, ctxs // 2
    tok, topk = routes_ref.shape
    ctx_tok = keys_ref.shape[0]
    per_dev = keys_ref.shape[1] // HD
    rows = tok * n
    seq = ctx_tok * ctxs
    width = w_hbm.shape[1]
    cw = ysend.shape[2]
    count = width // cw
    parts = w_sem.shape[0]
    sources = (keys_ref, values_ref)

    def at(head, ctx):
        return (head, ctx)

    sibling = chip * 2 + (1 - core)

    barrier = pltpu.get_barrier_semaphore()
    for i in range(1, n):
        pl.semaphore_signal(barrier, inc=1, device_id=at(lax.rem(me + i, n), cx), device_id_type=MESH)
    pl.semaphore_signal(barrier, inc=1, device_id=at(me, sibling), device_id_type=MESH)

    @pl.when(chip > 0)
    def _():
        pl.semaphore_signal(barrier, inc=1, device_id=at(me, cx - 2), device_id_type=MESH)

    @pl.when(chip < chips - 1)
    def _():
        pl.semaphore_signal(barrier, inc=1, device_id=at(me, cx + 2), device_id_type=MESH)

    def own_rows(c):
        return pl.ds(pl.multiple_of(c * ctx_tok, ctx_tok), ctx_tok)

    def head_cols(h):
        return pl.ds(pl.multiple_of(h * HD, HD), HD)

    def own_copy(a, h):
        return pltpu.make_async_copy(
            sources[a].at[:, head_cols(h)], kv.at[a, h, own_rows(cx), :], own_sem.at[a, h]
        )

    @pl.loop(0, per_dev)
    def _(h):
        for a in range(2):
            own_copy(a, h).start()

    depth = w_hbm.shape[0] // parts

    def w_copy(i):
        return pltpu.make_async_copy(
            w_hbm.at[i * depth:(i + 1) * depth, :], w_ref.at[i * depth:(i + 1) * depth, :], w_sem.at[i]
        )

    for k in range(topk):
        qf[k] = queries_ref[:, k * HD:(k + 1) * HD].astype(jnp.float32)
        rb[k] = jnp.broadcast_to(routes_ref[:, k:k + 1], (tok, HD))
        gb[k] = jnp.broadcast_to(gates_ref[:, k:k + 1], (tok, HD))

    pl.semaphore_wait(
        barrier, n + (chip > 0).astype(jnp.int32) + (chip < chips - 1).astype(jnp.int32)
    )

    def x_copy(a, h, k):
        block = kv.at[a, h, own_rows(k * 2 + core), :]
        return pltpu.make_async_remote_copy(
            src_ref=block, dst_ref=block, send_sem=x_send.at[a, h, k], recv_sem=x_recv.at[a, h, k],
            device_id=at(me, cx + 2), device_id_type=MESH,
        )

    def x_first(a, h):
        return pltpu.make_async_remote_copy(
            src_ref=sources[a].at[:, head_cols(h)], dst_ref=kv.at[a, h, own_rows(cx), :],
            send_sem=x_send.at[a, h, chips - 1], recv_sem=x_recv.at[a, h, chip],
            device_id=at(me, cx + 2), device_id_type=MESH,
        )

    def s_copy(a, h, k):
        block = kv.at[a, h, own_rows(k * 2 + core), :]
        return pltpu.make_async_remote_copy(
            src_ref=block, dst_ref=block, send_sem=s_send.at[a, h, k], recv_sem=s_recv.at[a, h, k],
            device_id=at(me, sibling), device_id_type=MESH,
        )

    def s_wait(a, h, k):
        block = kv.at[a, h, own_rows(k * 2 + (1 - core)), :]
        pltpu.make_async_remote_copy(
            src_ref=block, dst_ref=block, send_sem=s_send.at[a, h, k], recv_sem=s_recv.at[a, h, k],
            device_id=at(me, sibling), device_id_type=MESH,
        ).wait_recv()

    @pl.when(chip < chips - 1)
    def _():
        @pl.loop(0, per_dev)
        def _(h):
            for a in range(2):
                x_first(a, h).start()

    def slot_of(source, dest):
        return lax.rem(source + dest, 2) * m + source // 2

    def q_copy(i):
        dest = lax.rem(me + i, n)
        return pltpu.make_async_remote_copy(
            src_ref=qsend.at[i], dst_ref=qall.at[slot_of(me, dest)], send_sem=q_send.at[i], recv_sem=q_recv.at[i],
            device_id=at(dest, cx), device_id_type=MESH,
        )

    def g_copy(i):
        dest = lax.rem(me + i, n)
        return pltpu.make_async_remote_copy(
            src_ref=gsend.at[i], dst_ref=gall.at[slot_of(me, dest)], send_sem=g_send.at[i], recv_sem=g_recv.at[i],
            device_id=at(dest, cx), device_id_type=MESH,
        )

    def spread(i):
        first = lax.rem(me + i, n) * per_dev
        acc = [jnp.zeros((tok, HD), jnp.float32) for _ in range(per_dev)]
        gate = jnp.zeros((tok, HD), jnp.float32)
        lane = lax.broadcasted_iota(jnp.int32, (tok, HD), 1) + first
        for k in range(topk):
            head, q = rb[k], qf[k]
            for j in range(per_dev):
                acc[j] = jnp.where(head == first + j, q, acc[j])
            gate = jnp.where(head == lane, gb[k], gate)
        return jnp.concatenate([a.astype(jnp.bfloat16) for a in acc], axis=1), gate

    @pl.loop(1, n)
    def _(i):
        q, gate = spread(i)
        qsend[i] = q
        gsend[i] = gate
        q_copy(i).start()
        g_copy(i).start()

    for i in range(parts):
        w_copy(i).start()

    q, gate = spread(0)
    qall[z] = q
    gall[z] = gate

    @pl.loop(0, per_dev)
    def _(h):
        for a in range(2):
            own_copy(a, h).wait()
            s_copy(a, h, chip).start()

    @pl.loop(0, n)
    def _(slot):
        source = lax.rem(slot, m) * 2 + jnp.where(slot < m, y, 1 - y)
        base = cx * ctx_tok + source * tok
        qblock = base // BLK
        row = mask_ref[pl.ds(qblock, 1), :]
        kpos = lax.broadcasted_iota(jnp.int32, (tok, seq), 1)
        qpos = lax.broadcasted_iota(jnp.int32, (tok, seq), 0) + base
        kstart = qblock * BLK
        usable = ((row > 0.5) & (kpos < kstart)) | (kpos >= kstart)
        bias[pl.ds(pl.multiple_of(slot * tok, tok), tok), :] = jnp.where(
            usable & (kpos <= qpos), 0.0, -1e30
        ).astype(bias.dtype)

    @pl.loop(chip * 2 + 2, ctxs)
    def _(c):
        @pl.loop(0, per_dev)
        def _(h):
            for a in range(2):
                kv[a, h, own_rows(c), :] = jnp.zeros((ctx_tok, HD), jnp.bfloat16)

    @pl.loop(1, n)
    def _(i):
        source = lax.rem(me + n - i, n)
        slot = slot_of(source, me)
        pltpu.make_async_remote_copy(
            src_ref=qsend.at[i], dst_ref=qall.at[slot], send_sem=q_send.at[i], recv_sem=q_recv.at[i],
            device_id=at(source, cx), device_id_type=MESH,
        ).wait_recv()
        pltpu.make_async_remote_copy(
            src_ref=gsend.at[i], dst_ref=gall.at[slot], send_sem=g_send.at[i], recv_sem=g_recv.at[i],
            device_id=at(source, cx), device_id_type=MESH,
        ).wait_recv()

    scale = math.log2(math.e) / math.sqrt(HD)
    tile = max(tok, min(rows, (256 * 1024 // seq) // tok * tok))

    def forward(h):
        @pl.loop(0, chip)
        def _(k):
            for a in range(2):
                x_copy(a, h, k).wait_recv()
                s_copy(a, h, k).start()

            @pl.when(chip < chips - 1)
            def _():
                for a in range(2):
                    x_copy(a, h, k).start()

    def attend(h):
        @pl.loop(0, chip + 1)
        def _(k):
            for a in range(2):
                s_wait(a, h, k)

        def one(t):
            group = pl.ds(t * (tile // tok), tile // tok)
            here = pl.ds(pl.multiple_of(t * tile, tile), tile)
            q = qall[group, :, head_cols(h)].reshape(tile, HD)
            s = lax.dot_general(q, kv[0, h], (((1,), (1,)), ((), ())), preferred_element_type=jnp.float32)
            s = s * scale + bias[here, :].astype(jnp.float32)
            p = jnp.exp2(s - jnp.max(s, axis=1, keepdims=True))
            total = jnp.sum(p, axis=1, keepdims=True)
            o = jnp.dot(p.astype(jnp.bfloat16), kv[1, h], preferred_element_type=jnp.float32)
            lane = lax.broadcasted_iota(jnp.int32, (tile, HD), 1)
            gates = gall[group].reshape(tile, HD)
            g = jnp.sum(jnp.where(lane == h, gates, 0.0), axis=1, keepdims=True)
            weighted[here, head_cols(h)] = (o * (g / total)).astype(jnp.bfloat16)

        if rows == tile:
            one(0)
        else:
            pl.loop(0, rows // tile)(one)

    @pl.loop(0, per_dev + 1)
    def _(h):
        @pl.when(h < per_dev)
        def _():
            forward(h)

        @pl.when(h >= 1)
        def _():
            attend(h - 1)

    for i in range(parts):
        w_copy(i).wait()

    half = m * tok

    def y_copy(c):
        return pltpu.make_async_remote_copy(
            src_ref=ysend.at[c], dst_ref=yrecv.at[c], send_sem=y_send.at[c], recv_sem=y_recv.at[c],
            device_id=at(z * 2 + 1 - y, cx), device_id_type=MESH,
        )

    def up_copy(c, d):
        return pltpu.make_async_remote_copy(
            src_ref=psum.at[c, d], dst_ref=zrecv.at[c, d + 1], send_sem=up_send.at[c, d], recv_sem=up_recv.at[c, d],
            device_id=at(me + 2, cx), device_id_type=MESH,
        )

    def dn_copy(c, d):
        return pltpu.make_async_remote_copy(
            src_ref=psum.at[c, d], dst_ref=zrecv.at[c, d], send_sem=dn_send.at[c, d], recv_sem=dn_recv.at[c, d],
            device_id=at(me - 2, cx), device_id_type=MESH,
        )

    def add(c, d, got):
        psum[c, d] = (psum[c, d].astype(jnp.float32) + zrecv[c, got].astype(jnp.float32)).astype(jnp.bfloat16)

    @pl.loop(0, count + m)
    def _(i):
        @pl.when(i < count)
        def _():
            part = jnp.dot(
                weighted[...], w_ref[:, pl.ds(pl.multiple_of(i * cw, cw), cw)],
                preferred_element_type=jnp.float32,
            ).astype(jnp.bfloat16)
            ysend[i] = part[half:]
            psum[i] = part[:half].reshape(m, tok, cw)
            y_copy(i).start()

        @pl.when((i >= 1) & (i <= count))
        def _():
            c = i - 1
            y_copy(c).wait_recv()
            psum[c] = (
                psum[c].astype(jnp.float32) + yrecv[c].astype(jnp.float32).reshape(m, tok, cw)
            ).astype(jnp.bfloat16)

        cu = i - 1 - z
        cd = i - 1 - (m - 1 - z)

        @pl.when((cu >= 0) & (cu < count))
        def _():
            for d in range(m - 1, -1, -1):
                @pl.when((z > 0) & (z <= d))
                def _():
                    up_copy(cu, d).wait_recv()

                @pl.when(z < d)
                def _():
                    @pl.when(z > 0)
                    def _():
                        add(cu, d, d + 1)
                    up_copy(cu, d).start()

        @pl.when((cd >= 0) & (cd < count))
        def _():
            for d in range(m):
                @pl.when((z < m - 1) & (z >= d))
                def _():
                    dn_copy(cd, d).wait_recv()

                @pl.when(z > d)
                def _():
                    @pl.when(z < m - 1)
                    def _():
                        add(cd, d, d)
                    dn_copy(cd, d).start()

        @pl.when(i >= m)
        def _():
            c = i - m
            cols = pl.ds(pl.multiple_of(c * cw, cw), cw)
            for d in range(m):
                @pl.when(z == d)
                def _():
                    total = psum[c, d].astype(jnp.float32)
                    if d > 0:
                        total = total + zrecv[c, d + 1].astype(jnp.float32)
                    if d < m - 1:
                        total = total + zrecv[c, d].astype(jnp.float32)
                    out_ref[:, cols] = total.astype(jnp.bfloat16)

    @pl.loop(0, count)
    def _(c):
        y_copy(c).wait_send()
        for d in range(m):
            @pl.when(z < d)
            def _():
                up_copy(c, d).wait_send()

            @pl.when(z > d)
            def _():
                dn_copy(c, d).wait_send()

    @pl.loop(1, n)
    def _(i):
        q_copy(i).wait_send()
        g_copy(i).wait_send()

    @pl.loop(0, per_dev)
    def _(h):
        for a in range(2):
            @pl.loop(0, chip + 1)
            def _(k):
                s_copy(a, h, k).wait_send()

            @pl.when(chip < chips - 1)
            def _():
                x_first(a, h).wait_send()

                @pl.loop(0, chip)
                def _(k):
                    x_copy(a, h, k).wait_send()


def local(n, ctxs, queries, keys, values, routes, gates, block_mask, w_out):
    tok, topk = routes.shape
    ctx_tok, held = keys.shape
    per_dev = held // HD
    seq = ctx_tok * ctxs
    rows = tok * n
    depth, width = w_out.shape
    m = n // 2
    chips = ctxs // 2
    blocks = block_mask.shape[0]
    mask = jnp.broadcast_to(block_mask.astype(jnp.float32)[:, :, None], (blocks, blocks, BLK)).reshape(blocks, seq)
    count = width // CHUNK
    bf, f32, dma = jnp.bfloat16, jnp.float32, pltpu.SemaphoreType.DMA
    vmem = pl.BlockSpec(memory_space=pltpu.VMEM)
    hbm = pl.BlockSpec(memory_space=pl.ANY)
    return pl.pallas_call(
        functools.partial(kernel, n, ctxs),
        out_shape=jax.ShapeDtypeStruct((tok, width), bf),
        in_specs=[vmem, hbm, hbm, vmem, vmem, vmem, hbm],
        out_specs=vmem,
        scratch_shapes=[
            pltpu.VMEM((topk, tok, HD), f32),
            pltpu.VMEM((topk, tok, HD), jnp.int32),
            pltpu.VMEM((topk, tok, HD), f32),
            pltpu.VMEM((n, tok, held), bf),
            pltpu.VMEM((n, tok, HD), f32),
            pltpu.VMEM((n, tok, held), bf),
            pltpu.VMEM((n, tok, HD), f32),
            pltpu.VMEM((2, per_dev, seq, HD), bf),
            pltpu.VMEM((rows, seq), bf),
            pltpu.VMEM((rows, held), bf),
            pltpu.VMEM((depth, width), bf),
            pltpu.VMEM((count, m * tok, CHUNK), bf),
            pltpu.VMEM((count, m * tok, CHUNK), bf),
            pltpu.VMEM((count, m, tok, CHUNK), bf),
            pltpu.VMEM((count, m + 1, tok, CHUNK), bf),
            dma((8,)),
            dma((2, per_dev)),
            dma((2, per_dev, chips)),
            dma((2, per_dev, chips)),
            dma((2, per_dev, chips)),
            dma((2, per_dev, chips)),
            dma((n,)),
            dma((n,)),
            dma((n,)),
            dma((n,)),
            dma((count,)),
            dma((count,)),
            dma((count, m)),
            dma((count, m)),
            dma((count, m)),
            dma((count, m)),
        ],
        compiler_params=pltpu.CompilerParams(
            collective_id=0, has_side_effects=True, vmem_limit_bytes=63 * 1024 * 1024
        ),
    )(queries, keys, values, routes, gates, mask, w_out)


def solution(mesh):
    placed = (
        P(("ctx", "head"), None),
        P("ctx", "head"),
        P("ctx", "head"),
        P(("ctx", "head"), None),
        P(("ctx", "head"), None),
        P(),
        P("head", None),
    )
    return jax.shard_map(
        functools.partial(local, mesh.shape["head"], mesh.shape["ctx"]),
        mesh=mesh, in_specs=placed, out_specs=P(("ctx", "head"), None), check_vma=False,
    )
```

time: 244 us -> 104 us (0.43)
  Pallas kernels: 0 us -> 97.4 us
  waiting for transfers between devices: 87.3 us -> 0 us
  blocking collectives: 63.4 us -> 0 us
  matrix products: 26.8 us -> 0 us
  other arithmetic: 26.8 us -> 0.69 us
  between operations: 13.6 us -> 0.01 us
  local copies, waits for them, and re-layouts: 17.6 us -> 5.37 us
  starting transfers between devices: 6.01 us -> 0 us
    pallas_call x0 -> x1, Pallas kernels: none -> 97.4 us  [local(): pl.pallas_call(functools.partial(kernel, n, ctxs), out_shape=jax.ShapeDty...]
    reduce_scatter x1 -> x0, waiting for transfers between devices: 87.2 us -> none  [local(): lax.psum_scatter(jnp.dot(weighted, w_out, preferred_element_type=jnp.floa...]
    all_gather x2 -> x0, blocking collectives: 63.4 us -> none  [the longest x1 32.9 us: local(): lax.all_gather(routes, 'head', axis=0, tiled=True)]
    dot_general x7 -> x0, matrix products: 26.8 us -> none  [the longest x1 12.1 us: local(): jnp.dot(weighted, w_out, preferred_element_type=jnp.float32)]
    reduce_sum x8 -> x0, other arithmetic: 23.4 us -> none  [the longest x1 18.2 us: local(): jnp.sum(mapping * jnp.arange(ctx_tok, dtype=jnp.int32)[None, :, None], ax...]
    mul x6 -> x0, local copies, waits for them, and re-layouts: 7.09 us -> none  [the longest x4 6.94 us: local(): placed.transpose(2, 0, 1, 3)[:, :, :, None, :]]
    gather x3 -> x0, local copies, waits for them, and re-layouts: 6.92 us -> none  [the longest x2 3.68 us: update(): jnp.take(query_rows, key_pos // BLK, axis=2)]
    all_to_all x1 -> x0, starting transfers between devices: 5.97 us -> none  [local(): lax.all_to_all(packed, 'head', split_axis=0, concat_axis=2, tiled=True)]
  transfers between devices with their start and end apart: 3 -> 0, of which waited for: 1 -> 0; matrix products, arithmetic and copies ran while one was open for 15% -> 0% of each run, Pallas kernels for 0% -> 0%
where the time goes in v1:
time: 104 us; the launch traced here: 103 us
  Pallas kernels  97.4 us (94%)
  local copies, waits for them, and re-layouts  5.37 us (5%)
    pallas_call x1, Pallas kernels, local(): pl.pallas_call(functools.partial(kernel, n, ctxs), out_shape=jax.ShapeDty...  97.4 us
    unnamed x3, local copies, waits for them, and re-layouts  4.61 us

profile of v1, /device:TPU:2, one launch (start us, length us, event | category | flops | bytes accessed | tf_op | source)
XLA Modules:
  0.0 103.5 jit_solution(997430708932598230)
XLA Ops:
  0.0 0.7 convert_element_type.3
  0.7 0.1 copy.8
  0.8 1.4 %copy.9.routes_ref = s32[32,16]{1,0:T(8,128)} copy(s32[32,16]{0,1:T(8,128)} %param.10) | data formatting | bytes 4096 | tf_op args[3]
  2.1 1.4 %copy.10.gates_ref = f32[32,16]{1,0:T(8,128)} copy(f32[32,16]{0,1:T(8,128)} %param.11) | data formatting | bytes 4096 | tf_op args[4]
  3.5 0.7 broadcast_bitcast_fusion.mask_ref
  4.2 97.4 %shard_map.73 = bf16[32,8192]{1,0:T(8,128)(2,1)} custom-call(bf16[32,2048]{1,0:T(8,128)(2,1)} %queries_ref.1, bf16[256,1024]{1,0:T(8,128)(2,1)} %keys_ref.1, bf16[256,1024]{1,0:T(8,128)(2,1)} %values_ref.1, s32[32,16]{1,0:T(8,128)} %copy.9.routes_ref, f32[32,16]{1,0:T(8,128)} %copy.10.gates_ref, f32[8,1024]{1,0:T(8,128)} %broadcast_bitcast_fusion.mask_ref, ...), custom_call_target="tpu_custom_call" | custom-call | tf_op jit(solution)/shard_map/pallas_call | solution.py:399
  101.6 1.9 %copy.12 = bf16[32,8192]{1,0:T(8,128)(2,1)} copy(bf16[32,8192]{1,0:T(8,128)(2,1)} %shard_map.73) | data formatting | bytes 1048576

commit v2 on v1

--- a/solution.py
+++ b/solution.py
@@ -11,6 +11,7 @@
 HD = 128
 BLK = 128
 CHUNK = 512
+LAG = 4
 MESH = pl.DeviceIdType.MESH
 
 
@@ -18,7 +19,7 @@
     n, ctxs,
     queries_ref, keys_ref, values_ref, routes_ref, gates_ref, mask_ref, w_hbm,
     out_ref,
-    qf, rb, gb, qsend, gsend, qall, gall, kv, bias, weighted, w_ref,
+    mask_scr, qf, rb, gb, qsend, gsend, qall, gall, kv, bias, weighted, w_ref,
     ysend, yrecv, psum, zrecv,
     w_sem, own_sem, x_send, x_recv, s_send, s_recv, q_send, q_recv, g_send, g_recv,
     y_send, y_recv, up_send, up_recv, dn_send, dn_recv,
@@ -27,7 +28,7 @@
     cx = lax.axis_index("ctx")
     y, z, m = lax.rem(me, 2), me // 2, n // 2
     core, chip, chips = lax.rem(cx, 2), cx // 2, ctxs // 2
-    tok, topk = routes_ref.shape
+    topk, tok = routes_ref.shape
     ctx_tok = keys_ref.shape[0]
     per_dev = keys_ref.shape[1] // HD
     rows = tok * n
@@ -79,10 +80,16 @@
             w_hbm.at[i * depth:(i + 1) * depth, :], w_ref.at[i * depth:(i + 1) * depth, :], w_sem.at[i]
         )
 
+    routes = routes_ref[...].astype(jnp.float32).T.astype(jnp.int32)
+    gates = gates_ref[...].T
+    blocks = mask_ref.shape[0]
+    usable_blocks = mask_ref[...].astype(jnp.float32).T
+    for b in range(blocks):
+        mask_scr[:, b * BLK:(b + 1) * BLK] = jnp.broadcast_to(usable_blocks[:, b:b + 1], (blocks, BLK))
     for k in range(topk):
         qf[k] = queries_ref[:, k * HD:(k + 1) * HD].astype(jnp.float32)
-        rb[k] = jnp.broadcast_to(routes_ref[:, k:k + 1], (tok, HD))
-        gb[k] = jnp.broadcast_to(gates_ref[:, k:k + 1], (tok, HD))
+        rb[k] = jnp.broadcast_to(routes[:, k:k + 1], (tok, HD))
+        gb[k] = jnp.broadcast_to(gates[:, k:k + 1], (tok, HD))
 
     pl.semaphore_wait(
         barrier, n + (chip > 0).astype(jnp.int32) + (chip < chips - 1).astype(jnp.int32)
@@ -122,6 +129,9 @@
         def _(h):
             for a in range(2):
                 x_first(a, h).start()
+
+    for i in range(parts):
+        w_copy(i).start()
 
     def slot_of(source, dest):
         return lax.rem(source + dest, 2) * m + source // 2
@@ -160,9 +170,6 @@
         q_copy(i).start()
         g_copy(i).start()
 
-    for i in range(parts):
-        w_copy(i).start()
-
     q, gate = spread(0)
     qall[z] = q
     gall[z] = gate
@@ -178,7 +185,7 @@
         source = lax.rem(slot, m) * 2 + jnp.where(slot < m, y, 1 - y)
         base = cx * ctx_tok + source * tok
         qblock = base // BLK
-        row = mask_ref[pl.ds(qblock, 1), :]
+        row = mask_scr[pl.ds(qblock, 1), :]
         kpos = lax.broadcasted_iota(jnp.int32, (tok, seq), 1)
         qpos = lax.broadcasted_iota(jnp.int32, (tok, seq), 0) + base
         kstart = qblock * BLK
@@ -238,8 +245,8 @@
             total = jnp.sum(p, axis=1, keepdims=True)
             o = jnp.dot(p.astype(jnp.bfloat16), kv[1, h], preferred_element_type=jnp.float32)
             lane = lax.broadcasted_iota(jnp.int32, (tile, HD), 1)
-            gates = gall[group].reshape(tile, HD)
-            g = jnp.sum(jnp.where(lane == h, gates, 0.0), axis=1, keepdims=True)
+            gate = gall[group].reshape(tile, HD)
+            g = jnp.sum(jnp.where(lane == h, gate, 0.0), axis=1, keepdims=True)
             weighted[here, head_cols(h)] = (o * (g / total)).astype(jnp.bfloat16)
 
         if rows == tile:
@@ -283,7 +290,7 @@
     def add(c, d, got):
         psum[c, d] = (psum[c, d].astype(jnp.float32) + zrecv[c, got].astype(jnp.float32)).astype(jnp.bfloat16)
 
-    @pl.loop(0, count + m)
+    @pl.loop(0, count + m - 1 + LAG)
     def _(i):
         @pl.when(i < count)
         def _():
@@ -295,16 +302,16 @@
             psum[i] = part[:half].reshape(m, tok, cw)
             y_copy(i).start()
 
-        @pl.when((i >= 1) & (i <= count))
-        def _():
-            c = i - 1
+        @pl.when((i >= LAG) & (i < count + LAG))
+        def _():
+            c = i - LAG
             y_copy(c).wait_recv()
             psum[c] = (
                 psum[c].astype(jnp.float32) + yrecv[c].astype(jnp.float32).reshape(m, tok, cw)
             ).astype(jnp.bfloat16)
 
-        cu = i - 1 - z
-        cd = i - 1 - (m - 1 - z)
+        cu = i - LAG - z
+        cd = i - LAG - (m - 1 - z)
 
         @pl.when((cu >= 0) & (cu < count))
         def _():
@@ -334,9 +341,9 @@
                         add(cd, d, d)
                     dn_copy(cd, d).start()
 
-        @pl.when(i >= m)
-        def _():
-            c = i - m
+        @pl.when(i >= m - 1 + LAG)
+        def _():
+            c = i - (m - 1 + LAG)
             cols = pl.ds(pl.multiple_of(c * cw, cw), cw)
             for d in range(m):
                 @pl.when(z == d)
@@ -391,7 +398,6 @@
     m = n // 2
     chips = ctxs // 2
     blocks = block_mask.shape[0]
-    mask = jnp.broadcast_to(block_mask.astype(jnp.float32)[:, :, None], (blocks, blocks, BLK)).reshape(blocks, seq)
     count = width // CHUNK
     bf, f32, dma = jnp.bfloat16, jnp.float32, pltpu.SemaphoreType.DMA
     vmem = pl.BlockSpec(memory_space=pltpu.VMEM)
@@ -402,6 +408,7 @@
         in_specs=[vmem, hbm, hbm, vmem, vmem, vmem, hbm],
         out_specs=vmem,
         scratch_shapes=[
+            pltpu.VMEM((blocks, seq), f32),
             pltpu.VMEM((topk, tok, HD), f32),
             pltpu.VMEM((topk, tok, HD), jnp.int32),
             pltpu.VMEM((topk, tok, HD), f32),
@@ -437,7 +444,7 @@
         compiler_params=pltpu.CompilerParams(
             collective_id=0, has_side_effects=True, vmem_limit_bytes=63 * 1024 * 1024
         ),
-    )(queries, keys, values, routes, gates, mask, w_out)
+    )(queries, keys, values, routes.T, gates.T, block_mask.T, w_out)
 
 
 def solution(mesh):

time: 104 us -> 96.5 us (0.928)
  Pallas kernels: 97.4 us -> 93.1 us
  local copies, waits for them, and re-layouts: 5.37 us -> 3.22 us
    pallas_call x1, Pallas kernels: 97.4 us -> 93.1 us  [local(): pl.pallas_call(functools.partial(kernel, n, ctxs), out_shape=jax.ShapeDty...]
    unnamed x3 -> x2, local copies, waits for them, and re-layouts: 4.61 us -> 3.22 us
where the time goes in v2:
time: 96.5 us; the launch traced here: 96.3 us
  Pallas kernels  93.1 us (96%)
  local copies, waits for them, and re-layouts  3.22 us (3%)
    pallas_call x1, Pallas kernels, local(): pl.pallas_call(functools.partial(kernel, n, ctxs), out_shape=jax.ShapeDty...  93.1 us
    unnamed x2, local copies, waits for them, and re-layouts  3.22 us

profile of v2, /device:TPU:2, one launch (start us, length us, event | category | flops | bytes accessed | tf_op | source)
XLA Modules:
  0.0 96.3 jit_solution(11829965149176325234)
XLA Ops:
  0.0 1.3 %copy.8 = s32[8,8]{0,1:T(8,128)} copy(s32[8,8]{1,0:T(8,128)} %param.12) | data formatting | bytes 512 | tf_op args[5]
  1.3 93.1 %shard_map.73 = bf16[32,8192]{1,0:T(8,128)(2,1)} custom-call(bf16[32,2048]{1,0:T(8,128)(2,1)} %queries_ref.1, bf16[256,1024]{1,0:T(8,128)(2,1)} %keys_ref.1, bf16[256,1024]{1,0:T(8,128)(2,1)} %values_ref.1, s32[16,32]{1,0:T(8,128)} %bitcast.4, f32[16,32]{1,0:T(8,128)} %bitcast.5, s32[8,8]{1,0:T(8,128)} %bitcast.3, bf16[1024,8192]{1,0:T(8,128)(2,1)} %w_hbm.1), custom_call_target="tpu_custom_call" | custom-call | tf_op jit(solution)/shard_map/pallas_call | solution.py:405
  94.5 1.9 %copy.10 = bf16[32,8192]{1,0:T(8,128)(2,1)} copy(bf16[32,8192]{1,0:T(8,128)(2,1)} %shard_map.73) | data formatting | bytes 1048576

commit v3 on v2

--- a/solution.py
+++ b/solution.py
@@ -10,8 +10,8 @@
 
 HD = 128
 BLK = 128
-CHUNK = 512
-LAG = 4
+CHUNK = 1024
+LAG = 3
 MESH = pl.DeviceIdType.MESH
 
 
@@ -104,7 +104,7 @@
 
     def x_first(a, h):
         return pltpu.make_async_remote_copy(
-            src_ref=sources[a].at[:, head_cols(h)], dst_ref=kv.at[a, h, own_rows(cx), :],
+            src_ref=kv.at[a, h, own_rows(cx), :], dst_ref=kv.at[a, h, own_rows(cx), :],
             send_sem=x_send.at[a, h, chips - 1], recv_sem=x_recv.at[a, h, chip],
             device_id=at(me, cx + 2), device_id_type=MESH,
         )
@@ -123,12 +123,20 @@
             device_id=at(me, sibling), device_id_type=MESH,
         ).wait_recv()
 
-    @pl.when(chip < chips - 1)
-    def _():
-        @pl.loop(0, per_dev)
-        def _(h):
+    @pl.loop(0, per_dev)
+    def _(h):
+        for a in range(2):
+            own_copy(a, h).wait()
+
+        @pl.when(chip < chips - 1)
+        def _():
             for a in range(2):
                 x_first(a, h).start()
+
+    @pl.loop(0, per_dev)
+    def _(h):
+        for a in range(2):
+            s_copy(a, h, chip).start()
 
     for i in range(parts):
         w_copy(i).start()
@@ -173,12 +181,6 @@
     q, gate = spread(0)
     qall[z] = q
     gall[z] = gate
-
-    @pl.loop(0, per_dev)
-    def _(h):
-        for a in range(2):
-            own_copy(a, h).wait()
-            s_copy(a, h, chip).start()
 
     @pl.loop(0, n)
     def _(slot):

time: 96.5 us -> 96.6 us (level)
  no operation moved by 1% of the time
where the time goes in v3:
time: 96.6 us; the launch traced here: 96.4 us
  Pallas kernels  93.2 us (96%)
  local copies, waits for them, and re-layouts  3.22 us (3%)
    pallas_call x1, Pallas kernels, local(): pl.pallas_call(functools.partial(kernel, n, ctxs), out_shape=jax.ShapeDty...  93.2 us
    unnamed x2, local copies, waits for them, and re-layouts  3.22 us

profile of v3, /device:TPU:2, one launch (start us, length us, event | category | flops | bytes accessed | tf_op | source)
XLA Modules:
  0.0 96.4 jit_solution(15879199443948530994)
XLA Ops:
  0.0 1.3 %copy.8 = s32[8,8]{0,1:T(8,128)} copy(s32[8,8]{1,0:T(8,128)} %param.12) | data formatting | bytes 512 | tf_op args[5]
  1.3 93.2 %shard_map.73 = bf16[32,8192]{1,0:T(8,128)(2,1)} custom-call(bf16[32,2048]{1,0:T(8,128)(2,1)} %queries_ref.1, bf16[256,1024]{1,0:T(8,128)(2,1)} %keys_ref.1, bf16[256,1024]{1,0:T(8,128)(2,1)} %values_ref.1, s32[16,32]{1,0:T(8,128)} %bitcast.4, f32[16,32]{1,0:T(8,128)} %bitcast.5, s32[8,8]{1,0:T(8,128)} %bitcast.3, bf16[1024,8192]{1,0:T(8,128)(2,1)} %w_hbm.1), custom_call_target="tpu_custom_call" | custom-call | tf_op jit(solution)/shard_map/pallas_call | solution.py:407
  94.5 1.9 %copy.10 = bf16[32,8192]{1,0:T(8,128)(2,1)} copy(bf16[32,8192]{1,0:T(8,128)(2,1)} %shard_map.73) | data formatting | bytes 1048576
